TPU v7x, 512 devices: a whole 4x8x8 slice. The times are simulated.
512 devices in a mesh: sp: 128 (over y, z_lo, x, core), dp: 4 (over z_hi).
Axes of the slice: x: 4, y: 8, z: 8 (z_hi: 4, z_lo: 2; z = z_hi * 2 + z_lo), core: 2. Of those that a mesh axis runs over, the one named last changes fastest.
Arguments:
- queries: bfloat16 [32768, 5120], P(('sp', 'dp')), may hold values from -60 to 60
- keys: bfloat16 [32768, 1024], P(('sp', 'dp')), may hold values from -60 to 60
- values: bfloat16 [32768, 1024], P(('sp', 'dp')), may hold values from -6 to 6
- lengths: int32 [48], replicated, may hold values from 1 to 3840, 32768 in all
Outputs:
- attended: bfloat16 [32768, 5120], P(('sp', 'dp'))
Inputs may be any that keep to these rules, and one draw needn't show every extreme that they name: The lengths sum to 32768; the longest is exactly 3840.
All inputs are finite; a program needn't handle non-finite values.
Results may differ from a plain program's by a relative error of at most 0.0047.
Values may be sent and summed in bfloat16 or wider, within the bound.
No kernel may reach another device: no remote copies, remote signals or barrier semaphores. Data moves between devices by JAX's collectives and lax.ppermute only.
A program may use at most 64 MiB of HBM per device.

v0:
```python
import math

import jax
import jax.numpy as jnp
from jax import lax
from jax.sharding import PartitionSpec as P

HEAD_SIZE = 128


def shifted(block, axis, distance):
    devices = range(lax.axis_size(axis))
    route = [(i - distance, i) for i in devices if i - distance in devices]
    return lax.ppermute(block, axis, route)


def local(queries, keys, values, lengths):
    query_rows, key_rows, value_rows = (
        lax.all_to_all(queries, "dp", split_axis=1, concat_axis=0, tiled=True),
        lax.all_to_all(keys, "dp", split_axis=1, concat_axis=0, tiled=True),
        lax.all_to_all(values, "dp", split_axis=1, concat_axis=0, tiled=True),
    )
    row_count = query_rows.shape[0]
    query_heads = query_rows.shape[1] // HEAD_SIZE
    kv_heads = key_rows.shape[1] // HEAD_SIZE
    heads_per_group = query_heads // kv_heads
    level_count = min(4, lax.axis_size("sp") // 8 + 1)
    reach_blocks = 2**level_count - 1
    key_value = jnp.stack([key_rows, value_rows], 0)

    def advance(turn_index, state):
        current, stored = state
        current = shifted(current, "sp", 1)
        stored = lax.dynamic_update_index_in_dim(stored, current, turn_index, 0)
        return (current, stored)

    stored = jnp.zeros((reach_blocks + 1,) + key_value.shape, jnp.bfloat16).at[0].set(key_value)
    stored = lax.fori_loop(1, reach_blocks + 1, advance, (key_value, stored))[1]
    key_count = (reach_blocks + 1) * row_count
    keys_all = stored[:, 0].reshape(key_count, key_rows.shape[1])
    values_all = stored[:, 1].reshape(key_count, value_rows.shape[1])
    position = lax.axis_index("sp")
    doc_ends = jnp.cumsum(lengths)
    offsets = jnp.arange(row_count, dtype=jnp.int32)
    query_pos = position * row_count + offsets
    block_first = (position - jnp.arange(reach_blocks + 1, dtype=jnp.int32)) * row_count
    key_pos = (block_first[:, None] + offsets[None, :]).reshape(key_count)
    query_doc = jnp.sum((doc_ends[None, :] <= query_pos[:, None]).astype(jnp.int32), 1)
    key_doc = jnp.sum((doc_ends[None, :] <= key_pos[:, None]).astype(jnp.int32), 1)
    allowed = (
        (key_pos[None, :] <= query_pos[:, None])
        & (key_pos[None, :] >= 0)
        & (key_doc[None, :] == query_doc[:, None])
    )
    scaling = 1.0 / math.sqrt(HEAD_SIZE)

    def one_head(head_index):
        query_cols = lax.dynamic_slice_in_dim(query_rows, head_index * HEAD_SIZE, HEAD_SIZE, 1)
        kv_index = head_index // heads_per_group
        key_cols = lax.dynamic_slice_in_dim(keys_all, kv_index * HEAD_SIZE, HEAD_SIZE, 1)
        value_cols = lax.dynamic_slice_in_dim(values_all, kv_index * HEAD_SIZE, HEAD_SIZE, 1)
        scores = (
            lax.dot_general(
                query_cols, key_cols, (((1,), (1,)), ((), ())), preferred_element_type=jnp.float32
            )
            * scaling
        )
        scores = jnp.where(allowed, scores, -jnp.inf)
        row_max = jnp.max(scores, -1, keepdims=True)
        raw_weights = jnp.exp(scores - row_max)
        weights = (raw_weights / jnp.sum(raw_weights, -1, keepdims=True)).astype(jnp.bfloat16)
        return jnp.dot(weights, value_cols, preferred_element_type=jnp.float32).astype(jnp.bfloat16)

    outputs = lax.map(one_head, jnp.arange(query_heads, dtype=jnp.int32))
    merged = jnp.moveaxis(outputs, 0, 1).reshape(row_count, query_heads * HEAD_SIZE)
    return lax.all_to_all(merged, "dp", split_axis=0, concat_axis=1, tiled=True)


def solution(mesh):
    in_specs = (P(("sp", "dp"), None), P(("sp", "dp"), None), P(("sp", "dp"), None), P())
    out_specs = P(("sp", "dp"), None)
    return jax.shard_map(local, mesh=mesh, in_specs=in_specs, out_specs=out_specs, check_vma=False)
```

profile of v0, /device:TPU:32, one launch (start us, length us, event | category | flops | bytes accessed | tf_op | source)
XLA Modules:
  0.0 334.2 jit_solution(4685876080725462007)
XLA Ops:
  1.6 10.3 %all-to-all-start.1 = ((bf16[64,4,256]{2,0,1:T(8,128)(2,1)}), bf16[64,4,256]{2,0,1:T(8,128)(2,1)S(1)}, u32[]{:S(2)}, u32[]{:S(2)}) async-start(bf16[64,4,256]{2,0,1:T(8,128)(2,1)} %bitcast.41), calls=%async_computation.1 | async-start | bytes 262144 | tf_op jit(solution)/shard_map/all_to_all | solution.py:20
  16.7 4.4 %all-to-all-done.1 = bf16[64,4,256]{2,0,1:T(8,128)(2,1)S(1)} async-done(((bf16[64,4,256]{2,0,1:T(8,128)(2,1)}), bf16[64,4,256]{2,0,1:T(8,128)(2,1)S(1)}, u32[]{:S(2)}, u32[]{:S(2)}) %all-to-all-start.1) | async-done | bytes 131104 | tf_op jit(solution)/shard_map/all_to_all | solution.py:20
  21.1 3.3 all-to-all-start.2
  24.5 8.7 %all-to-all-done.2 = bf16[64,4,256]{2,0,1:T(8,128)(2,1)S(1)} async-done(((bf16[64,4,256]{2,0,1:T(8,128)(2,1)}), bf16[64,4,256]{2,0,1:T(8,128)(2,1)S(1)}, u32[]{:S(2)}, u32[]{:S(2)}) %all-to-all-start.2) | async-done | bytes 131104 | tf_op jit(solution)/shard_map/all_to_all | solution.py:21
  33.2 3.5 %all-to-all-start = ((bf16[64,4,1280]{2,0,1:T(8,128)(2,1)}), bf16[64,4,1280]{2,0,1:T(8,128)(2,1)S(1)}, u32[]{:S(2)}, u32[]{:S(2)}) async-start(bf16[64,4,1280]{2,0,1:T(8,128)(2,1)} %bitcast.39), calls=%async_computation | async-start | bytes 1310720 | tf_op jit(solution)/shard_map/all_to_all | solution.py:19
  39.1 191.7 %while.29 = (s32[]{:T(128)}, bf16[2,256,256]{2,1,0:T(8,128)(2,1)S(1)}, bf16[16,2,256,256]{3,2,1,0:T(8,128)(2,1)}, s32[]{:T(128)}, s32[]{:T(128)}, /*index=5*/s32[]{:T(128)}) while((s32[]{:T(128)}, bf16[2,256,256]{2,1,0:T(8,128)(2,1)S(1)}, bf16[16,2,256,256]{3,2,1,0:T(8,128)(2,1)}, s32[]{:T(128)}, s32[]{:T(128)}, /*index=5*/s32[]{:T(128)}) %tuple.61), condition=%wide.region_1.2_spmd, body=%wide.region_0.0_spmd.sunk | while | flops 5 | bytes 2097307 | solution.py:38
  41.0 11.9 %collective-permute-done = bf16[2,256,256]{2,1,0:T(8,128)(2,1)S(1)} collective-permute-done((bf16[2,256,256]{2,1,0:T(8,128)(2,1)S(1)}, bf16[2,256,256]{2,1,0:T(8,128)(2,1)S(1)}, u32[]{:S(2)}, u32[]{:S(2)}) %collective-permute-start) | collective-permute-done | bytes 262176 | tf_op jit(solution)/shard_map/while/body/eval_jaxpr/ppermute | solution.py:14
  55.6 10.0 %collective-permute-done = bf16[2,256,256]{2,1,0:T(8,128)(2,1)S(1)} collective-permute-done((bf16[2,256,256]{2,1,0:T(8,128)(2,1)S(1)}, bf16[2,256,256]{2,1,0:T(8,128)(2,1)S(1)}, u32[]{:S(2)}, u32[]{:S(2)}) %collective-permute-start) | collective-permute-done | bytes 262176 | tf_op jit(solution)/shard_map/while/body/eval_jaxpr/ppermute | solution.py:14
  68.3 10.0 %collective-permute-done = bf16[2,256,256]{2,1,0:T(8,128)(2,1)S(1)} collective-permute-done((bf16[2,256,256]{2,1,0:T(8,128)(2,1)S(1)}, bf16[2,256,256]{2,1,0:T(8,128)(2,1)S(1)}, u32[]{:S(2)}, u32[]{:S(2)}) %collective-permute-start) | collective-permute-done | bytes 262176 | tf_op jit(solution)/shard_map/while/body/eval_jaxpr/ppermute | solution.py:14
  80.9 10.0 %collective-permute-done = bf16[2,256,256]{2,1,0:T(8,128)(2,1)S(1)} collective-permute-done((bf16[2,256,256]{2,1,0:T(8,128)(2,1)S(1)}, bf16[2,256,256]{2,1,0:T(8,128)(2,1)S(1)}, u32[]{:S(2)}, u32[]{:S(2)}) %collective-permute-start) | collective-permute-done | bytes 262176 | tf_op jit(solution)/shard_map/while/body/eval_jaxpr/ppermute | solution.py:14
  93.6 10.0 %collective-permute-done = bf16[2,256,256]{2,1,0:T(8,128)(2,1)S(1)} collective-permute-done((bf16[2,256,256]{2,1,0:T(8,128)(2,1)S(1)}, bf16[2,256,256]{2,1,0:T(8,128)(2,1)S(1)}, u32[]{:S(2)}, u32[]{:S(2)}) %collective-permute-start) | collective-permute-done | bytes 262176 | tf_op jit(solution)/shard_map/while/body/eval_jaxpr/ppermute | solution.py:14
  106.3 10.0 %collective-permute-done = bf16[2,256,256]{2,1,0:T(8,128)(2,1)S(1)} collective-permute-done((bf16[2,256,256]{2,1,0:T(8,128)(2,1)S(1)}, bf16[2,256,256]{2,1,0:T(8,128)(2,1)S(1)}, u32[]{:S(2)}, u32[]{:S(2)}) %collective-permute-start) | collective-permute-done | bytes 262176 | tf_op jit(solution)/shard_map/while/body/eval_jaxpr/ppermute | solution.py:14
  118.9 10.0 %collective-permute-done = bf16[2,256,256]{2,1,0:T(8,128)(2,1)S(1)} collective-permute-done((bf16[2,256,256]{2,1,0:T(8,128)(2,1)S(1)}, bf16[2,256,256]{2,1,0:T(8,128)(2,1)S(1)}, u32[]{:S(2)}, u32[]{:S(2)}) %collective-permute-start) | collective-permute-done | bytes 262176 | tf_op jit(solution)/shard_map/while/body/eval_jaxpr/ppermute | solution.py:14
  131.6 10.0 %collective-permute-done = bf16[2,256,256]{2,1,0:T(8,128)(2,1)S(1)} collective-permute-done((bf16[2,256,256]{2,1,0:T(8,128)(2,1)S(1)}, bf16[2,256,256]{2,1,0:T(8,128)(2,1)S(1)}, u32[]{:S(2)}, u32[]{:S(2)}) %collective-permute-start) | collective-permute-done | bytes 262176 | tf_op jit(solution)/shard_map/while/body/eval_jaxpr/ppermute | solution.py:14
  144.2 10.0 %collective-permute-done = bf16[2,256,256]{2,1,0:T(8,128)(2,1)S(1)} collective-permute-done((bf16[2,256,256]{2,1,0:T(8,128)(2,1)S(1)}, bf16[2,256,256]{2,1,0:T(8,128)(2,1)S(1)}, u32[]{:S(2)}, u32[]{:S(2)}) %collective-permute-start) | collective-permute-done | bytes 262176 | tf_op jit(solution)/shard_map/while/body/eval_jaxpr/ppermute | solution.py:14
  156.9 10.0 %collective-permute-done = bf16[2,256,256]{2,1,0:T(8,128)(2,1)S(1)} collective-permute-done((bf16[2,256,256]{2,1,0:T(8,128)(2,1)S(1)}, bf16[2,256,256]{2,1,0:T(8,128)(2,1)S(1)}, u32[]{:S(2)}, u32[]{:S(2)}) %collective-permute-start) | collective-permute-done | bytes 262176 | tf_op jit(solution)/shard_map/while/body/eval_jaxpr/ppermute | solution.py:14
  169.5 10.0 %collective-permute-done = bf16[2,256,256]{2,1,0:T(8,128)(2,1)S(1)} collective-permute-done((bf16[2,256,256]{2,1,0:T(8,128)(2,1)S(1)}, bf16[2,256,256]{2,1,0:T(8,128)(2,1)S(1)}, u32[]{:S(2)}, u32[]{:S(2)}) %collective-permute-start) | collective-permute-done | bytes 262176 | tf_op jit(solution)/shard_map/while/body/eval_jaxpr/ppermute | solution.py:14
  182.2 10.0 %collective-permute-done = bf16[2,256,256]{2,1,0:T(8,128)(2,1)S(1)} collective-permute-done((bf16[2,256,256]{2,1,0:T(8,128)(2,1)S(1)}, bf16[2,256,256]{2,1,0:T(8,128)(2,1)S(1)}, u32[]{:S(2)}, u32[]{:S(2)}) %collective-permute-start) | collective-permute-done | bytes 262176 | tf_op jit(solution)/shard_map/while/body/eval_jaxpr/ppermute | solution.py:14
  194.8 10.0 %collective-permute-done = bf16[2,256,256]{2,1,0:T(8,128)(2,1)S(1)} collective-permute-done((bf16[2,256,256]{2,1,0:T(8,128)(2,1)S(1)}, bf16[2,256,256]{2,1,0:T(8,128)(2,1)S(1)}, u32[]{:S(2)}, u32[]{:S(2)}) %collective-permute-start) | collective-permute-done | bytes 262176 | tf_op jit(solution)/shard_map/while/body/eval_jaxpr/ppermute | solution.py:14
  207.5 10.0 %collective-permute-done = bf16[2,256,256]{2,1,0:T(8,128)(2,1)S(1)} collective-permute-done((bf16[2,256,256]{2,1,0:T(8,128)(2,1)S(1)}, bf16[2,256,256]{2,1,0:T(8,128)(2,1)S(1)}, u32[]{:S(2)}, u32[]{:S(2)}) %collective-permute-start) | collective-permute-done | bytes 262176 | tf_op jit(solution)/shard_map/while/body/eval_jaxpr/ppermute | solution.py:14
  220.1 10.0 %collective-permute-done = bf16[2,256,256]{2,1,0:T(8,128)(2,1)S(1)} collective-permute-done((bf16[2,256,256]{2,1,0:T(8,128)(2,1)S(1)}, bf16[2,256,256]{2,1,0:T(8,128)(2,1)S(1)}, u32[]{:S(2)}, u32[]{:S(2)}) %collective-permute-start) | collective-permute-done | bytes 262176 | tf_op jit(solution)/shard_map/while/body/eval_jaxpr/ppermute | solution.py:14
  230.9 3.9 %fusion.15 = (bf16[16,1,256,256]{3,2,1,0:T(8,128)(2,1)S(1)}, bf16[16,1,256,256]{3,2,1,0:T(8,128)(2,1)}) fusion(bf16[16,2,256,256]{3,2,1,0:T(8,128)(2,1)} %get-tuple-element.171), kind=kLoop, calls=%fused_computation.28 | loop fusion | bytes 8388608 | tf_op jit(solution)/shard_map/slice | solution.py:41
  234.8 79.1 %while.30 = (s32[]{:T(128)}, bf16[10,256,128]{2,1,0:T(8,128)(2,1)S(1)}, s32[10]{0:T(128)S(1)}, bf16[256,1280]{1,0:T(8,128)(2,1)S(1)}, bf16[4096,256]{1,0:T(8,128...) while((s32[]{:T(128)}, ...), condition=%wide.region_8.9_spmd.clone, body=%wide.region_5.8_spmd.clone.sunk | while | flops 549486080 | bytes 14855555 | solution.py:74
  314.8 18.5 %all_to_all.70 = bf16[4,64,1280]{2,1,0:T(8,128)(2,1)S(1)} all-to-all(bf16[4,64,1280]{2,1,0:T(8,128)(2,1)S(1)} %all_to_all.62), channel_id=1, replica_groups=mesh['sp'=128,'dp'=4] {'dp'}, dimensions={0} | all-to-all | bytes 1310720 | tf_op jit(solution)/shard_map/all_to_all | solution.py:76
  (106 shorter events, 103.2 us)
Async XLA Ops:
  1.6 19.6 %all-to-all-start.1 = ((bf16[64,4,256]{2,0,1:T(8,128)(2,1)}), bf16[64,4,256]{2,0,1:T(8,128)(2,1)S(1)}, u32[]{:S(2)}, u32[]{:S(2)}) async-start(bf16[64,4,256]{2,0,1:T(8,128)(2,1)} %bitcast.41), calls=%async_computation.1 | async-start | bytes 262144 | tf_op jit(solution)/shard_map/all_to_all | solution.py:20
  21.1 12.1 %all-to-all-start.2 = ((bf16[64,4,256]{2,0,1:T(8,128)(2,1)}), bf16[64,4,256]{2,0,1:T(8,128)(2,1)S(1)}, u32[]{:S(2)}, u32[]{:S(2)}) async-start(bf16[64,4,256]{2,0,1:T(8,128)(2,1)} %bitcast.40), calls=%async_computation.2 | async-start | bytes 262144 | tf_op jit(solution)/shard_map/all_to_all | solution.py:21
  33.2 201.6 %all-to-all-start = ((bf16[64,4,1280]{2,0,1:T(8,128)(2,1)}), bf16[64,4,1280]{2,0,1:T(8,128)(2,1)S(1)}, u32[]{:S(2)}, u32[]{:S(2)}) async-start(bf16[64,4,1280]{2,0,1:T(8,128)(2,1)} %bitcast.39), calls=%async_computation | async-start | bytes 1310720 | tf_op jit(solution)/shard_map/all_to_all | solution.py:19
  39.1 13.8 %collective-permute-start = (bf16[2,256,256]{2,1,0:T(8,128)(2,1)S(1)}, bf16[2,256,256]{2,1,0:T(8,128)(2,1)S(1)}, u32[]{:S(2)}, u32[]{:S(2)}) collective-permute-start(bf16[2,256,256]{2,1,0:T(8,128)(2,1)S(1)} %get-tuple-element.333), channel_id=1, source_target_pairs={{0,4},{4,8},{8,12},{12,16},{16,20},{20,24},{24,28},{28,32},{32,36}... | collective-permute-start | bytes 786440 | tf_op jit(solution)/shard_map/while/body/eval_jaxpr/ppermute | solution.py:14
  53.7 11.9 %collective-permute-start = (bf16[2,256,256]{2,1,0:T(8,128)(2,1)S(1)}, bf16[2,256,256]{2,1,0:T(8,128)(2,1)S(1)}, u32[]{:S(2)}, u32[]{:S(2)}) collective-permute-start(bf16[2,256,256]{2,1,0:T(8,128)(2,1)S(1)} %get-tuple-element.333), channel_id=1, source_target_pairs={{0,4},{4,8},{8,12},{12,16},{16,20},{20,24},{24,28},{28,32},{32,36}... | collective-permute-start | bytes 786440 | tf_op jit(solution)/shard_map/while/body/eval_jaxpr/ppermute | solution.py:14
  66.4 11.9 %collective-permute-start = (bf16[2,256,256]{2,1,0:T(8,128)(2,1)S(1)}, bf16[2,256,256]{2,1,0:T(8,128)(2,1)S(1)}, u32[]{:S(2)}, u32[]{:S(2)}) collective-permute-start(bf16[2,256,256]{2,1,0:T(8,128)(2,1)S(1)} %get-tuple-element.333), channel_id=1, source_target_pairs={{0,4},{4,8},{8,12},{12,16},{16,20},{20,24},{24,28},{28,32},{32,36}... | collective-permute-start | bytes 786440 | tf_op jit(solution)/shard_map/while/body/eval_jaxpr/ppermute | solution.py:14
  79.0 11.9 %collective-permute-start = (bf16[2,256,256]{2,1,0:T(8,128)(2,1)S(1)}, bf16[2,256,256]{2,1,0:T(8,128)(2,1)S(1)}, u32[]{:S(2)}, u32[]{:S(2)}) collective-permute-start(bf16[2,256,256]{2,1,0:T(8,128)(2,1)S(1)} %get-tuple-element.333), channel_id=1, source_target_pairs={{0,4},{4,8},{8,12},{12,16},{16,20},{20,24},{24,28},{28,32},{32,36}... | collective-permute-start | bytes 786440 | tf_op jit(solution)/shard_map/while/body/eval_jaxpr/ppermute | solution.py:14
  91.7 11.9 %collective-permute-start = (bf16[2,256,256]{2,1,0:T(8,128)(2,1)S(1)}, bf16[2,256,256]{2,1,0:T(8,128)(2,1)S(1)}, u32[]{:S(2)}, u32[]{:S(2)}) collective-permute-start(bf16[2,256,256]{2,1,0:T(8,128)(2,1)S(1)} %get-tuple-element.333), channel_id=1, source_target_pairs={{0,4},{4,8},{8,12},{12,16},{16,20},{20,24},{24,28},{28,32},{32,36}... | collective-permute-start | bytes 786440 | tf_op jit(solution)/shard_map/while/body/eval_jaxpr/ppermute | solution.py:14
  104.3 11.9 %collective-permute-start = (bf16[2,256,256]{2,1,0:T(8,128)(2,1)S(1)}, bf16[2,256,256]{2,1,0:T(8,128)(2,1)S(1)}, u32[]{:S(2)}, u32[]{:S(2)}) collective-permute-start(bf16[2,256,256]{2,1,0:T(8,128)(2,1)S(1)} %get-tuple-element.333), channel_id=1, source_target_pairs={{0,4},{4,8},{8,12},{12,16},{16,20},{20,24},{24,28},{28,32},{32,36}... | collective-permute-start | bytes 786440 | tf_op jit(solution)/shard_map/while/body/eval_jaxpr/ppermute | solution.py:14
  117.0 11.9 %collective-permute-start = (bf16[2,256,256]{2,1,0:T(8,128)(2,1)S(1)}, bf16[2,256,256]{2,1,0:T(8,128)(2,1)S(1)}, u32[]{:S(2)}, u32[]{:S(2)}) collective-permute-start(bf16[2,256,256]{2,1,0:T(8,128)(2,1)S(1)} %get-tuple-element.333), channel_id=1, source_target_pairs={{0,4},{4,8},{8,12},{12,16},{16,20},{20,24},{24,28},{28,32},{32,36}... | collective-permute-start | bytes 786440 | tf_op jit(solution)/shard_map/while/body/eval_jaxpr/ppermute | solution.py:14
  129.6 11.9 %collective-permute-start = (bf16[2,256,256]{2,1,0:T(8,128)(2,1)S(1)}, bf16[2,256,256]{2,1,0:T(8,128)(2,1)S(1)}, u32[]{:S(2)}, u32[]{:S(2)}) collective-permute-start(bf16[2,256,256]{2,1,0:T(8,128)(2,1)S(1)} %get-tuple-element.333), channel_id=1, source_target_pairs={{0,4},{4,8},{8,12},{12,16},{16,20},{20,24},{24,28},{28,32},{32,36}... | collective-permute-start | bytes 786440 | tf_op jit(solution)/shard_map/while/body/eval_jaxpr/ppermute | solution.py:14
  142.3 11.9 %collective-permute-start = (bf16[2,256,256]{2,1,0:T(8,128)(2,1)S(1)}, bf16[2,256,256]{2,1,0:T(8,128)(2,1)S(1)}, u32[]{:S(2)}, u32[]{:S(2)}) collective-permute-start(bf16[2,256,256]{2,1,0:T(8,128)(2,1)S(1)} %get-tuple-element.333), channel_id=1, source_target_pairs={{0,4},{4,8},{8,12},{12,16},{16,20},{20,24},{24,28},{28,32},{32,36}... | collective-permute-start | bytes 786440 | tf_op jit(solution)/shard_map/while/body/eval_jaxpr/ppermute | solution.py:14
  154.9 11.9 %collective-permute-start = (bf16[2,256,256]{2,1,0:T(8,128)(2,1)S(1)}, bf16[2,256,256]{2,1,0:T(8,128)(2,1)S(1)}, u32[]{:S(2)}, u32[]{:S(2)}) collective-permute-start(bf16[2,256,256]{2,1,0:T(8,128)(2,1)S(1)} %get-tuple-element.333), channel_id=1, source_target_pairs={{0,4},{4,8},{8,12},{12,16},{16,20},{20,24},{24,28},{28,32},{32,36}... | collective-permute-start | bytes 786440 | tf_op jit(solution)/shard_map/while/body/eval_jaxpr/ppermute | solution.py:14
  167.6 11.9 %collective-permute-start = (bf16[2,256,256]{2,1,0:T(8,128)(2,1)S(1)}, bf16[2,256,256]{2,1,0:T(8,128)(2,1)S(1)}, u32[]{:S(2)}, u32[]{:S(2)}) collective-permute-start(bf16[2,256,256]{2,1,0:T(8,128)(2,1)S(1)} %get-tuple-element.333), channel_id=1, source_target_pairs={{0,4},{4,8},{8,12},{12,16},{16,20},{20,24},{24,28},{28,32},{32,36}... | collective-permute-start | bytes 786440 | tf_op jit(solution)/shard_map/while/body/eval_jaxpr/ppermute | solution.py:14
  180.2 11.9 %collective-permute-start = (bf16[2,256,256]{2,1,0:T(8,128)(2,1)S(1)}, bf16[2,256,256]{2,1,0:T(8,128)(2,1)S(1)}, u32[]{:S(2)}, u32[]{:S(2)}) collective-permute-start(bf16[2,256,256]{2,1,0:T(8,128)(2,1)S(1)} %get-tuple-element.333), channel_id=1, source_target_pairs={{0,4},{4,8},{8,12},{12,16},{16,20},{20,24},{24,28},{28,32},{32,36}... | collective-permute-start | bytes 786440 | tf_op jit(solution)/shard_map/while/body/eval_jaxpr/ppermute | solution.py:14
  192.9 11.9 %collective-permute-start = (bf16[2,256,256]{2,1,0:T(8,128)(2,1)S(1)}, bf16[2,256,256]{2,1,0:T(8,128)(2,1)S(1)}, u32[]{:S(2)}, u32[]{:S(2)}) collective-permute-start(bf16[2,256,256]{2,1,0:T(8,128)(2,1)S(1)} %get-tuple-element.333), channel_id=1, source_target_pairs={{0,4},{4,8},{8,12},{12,16},{16,20},{20,24},{24,28},{28,32},{32,36}... | collective-permute-start | bytes 786440 | tf_op jit(solution)/shard_map/while/body/eval_jaxpr/ppermute | solution.py:14
  205.6 11.9 %collective-permute-start = (bf16[2,256,256]{2,1,0:T(8,128)(2,1)S(1)}, bf16[2,256,256]{2,1,0:T(8,128)(2,1)S(1)}, u32[]{:S(2)}, u32[]{:S(2)}) collective-permute-start(bf16[2,256,256]{2,1,0:T(8,128)(2,1)S(1)} %get-tuple-element.333), channel_id=1, source_target_pairs={{0,4},{4,8},{8,12},{12,16},{16,20},{20,24},{24,28},{28,32},{32,36}... | collective-permute-start | bytes 786440 | tf_op jit(solution)/shard_map/while/body/eval_jaxpr/ppermute | solution.py:14
  218.2 11.9 %collective-permute-start = (bf16[2,256,256]{2,1,0:T(8,128)(2,1)S(1)}, bf16[2,256,256]{2,1,0:T(8,128)(2,1)S(1)}, u32[]{:S(2)}, u32[]{:S(2)}) collective-permute-start(bf16[2,256,256]{2,1,0:T(8,128)(2,1)S(1)} %get-tuple-element.333), channel_id=1, source_target_pairs={{0,4},{4,8},{8,12},{12,16},{16,20},{20,24},{24,28},{28,32},{32,36}... | collective-permute-start | bytes 786440 | tf_op jit(solution)/shard_map/while/body/eval_jaxpr/ppermute | solution.py:14
where the time goes:
time: 336 us; the launch traced here: 334 us
  waiting for transfers between devices  165 us (49%)
  starting transfers between devices  45.7 us (14%)
  matrix products  39.7 us (12%)
  local copies, waits for them, and re-layouts  31 us (9%)
  loops' own time  26.6 us (8%)
  blocking collectives  18.5 us (6%)
  other arithmetic  7.75 us (2%)
    ppermute x15, waiting for transfers between devices, shifted(): return lax.ppermute(block, axis, route)  152 us
    dot_general x10, matrix products, one_head(): lax.dot_general(query_cols, key_cols, (((1,), (1,)), ((), ())), preferred...  29 us
    ppermute x15, starting transfers between devices, shifted(): return lax.ppermute(block, axis, route)  28.6 us
    another operation x1, loops' own time, local(): outputs = lax.map(one_head, jnp.arange(query_heads, dtype=jnp.int32))  26.3 us
    all_to_all x1, blocking collectives, local(): return lax.all_to_all(merged, 'dp', split_axis=0, concat_axis=1, tiled=True)  18.5 us
    dynamic_update_slice x15, local copies, waits for them, and re-layouts, advance(): stored = lax.dynamic_update_index_in_dim(stored, current, turn_index, 0)  11 us
    dot_general x10, matrix products, one_head(): jnp.dot(weights, value_cols, preferred_element_type=jnp.float32)  10.7 us
    all_to_all x1, starting transfers between devices, local(): lax.all_to_all(keys, 'dp', split_axis=1, concat_axis=0, tiled=True)  10.3 us
  transfers between devices with their start and end apart: 18, of which 17 were waited for; matrix products, arithmetic and copies ran while one was open for 7% of the time, Pallas kernels for 0%

commit v1 on v0

v1 whole, which is shorter than its diff:
```python
import functools
import math

import jax
import jax.numpy as jnp
from jax import lax
from jax.experimental import pallas as pl
from jax.experimental.pallas import tpu as pltpu
from jax.sharding import Mesh, PartitionSpec as P

HEAD = 128
HEADS = 40
GROUPS = 8
PER_GROUP = HEADS // GROUPS
TILE = 256
BACK = 4
TILES = 2 * (BACK + 1)
SUPER = 1024
SCALE = math.log2(math.e) / math.sqrt(HEAD)
LOWEST = -1e30


def attend(scalars, q_ref, lows_ref, own_refs, other_refs, out_ref, kt_s, v_s, m_s, acc_s):
    for source, refs in enumerate((own_refs, other_refs)):
        for block, ref in enumerate(refs):
            for half in range(2):
                place = source * TILES + 2 * block + half
                rows = slice(half * TILE, (half + 1) * TILE)
                kt_s[place] = ref[rows, :HEAD].T
                v_s[place, :, :HEAD] = ref[rows, HEAD:]
                v_s[place, :, HEAD:] = jnp.ones((TILE, HEAD), jnp.bfloat16)

    for block in range(2):
        first = scalars[block]
        low_first = scalars[2 + block]
        low_last = scalars[4 + block]
        m_s[...] = jnp.full(m_s.shape, LOWEST, jnp.float32)
        acc_s[...] = jnp.zeros(acc_s.shape, jnp.float32)
        rows = slice(block * TILE, (block + 1) * TILE)

        def visit(place, allowed):
            kt = kt_s[place]
            v = v_s[place]
            for head in range(PER_GROUP):
                q = q_ref[rows, head * HEAD : (head + 1) * HEAD]
                scores = jnp.dot(q, kt, preferred_element_type=jnp.float32) * SCALE
                if allowed is not None:
                    scores = jnp.where(allowed, scores, LOWEST)
                m_old = m_s[head]
                m_new = jnp.maximum(m_old, jnp.max(scores, 1, keepdims=True))
                m_s[head] = m_new
                alpha = jnp.exp2(m_old - m_new)
                weights = jnp.exp2(scores - jnp.concatenate([m_new, m_new], 1)).astype(jnp.bfloat16)
                part = jnp.dot(weights, v, preferred_element_type=jnp.float32)
                acc_s[head] = acc_s[head] * jnp.concatenate([alpha, alpha], 1) + part

        for source in range(2):
            base = scalars[6 + source]
            start = jnp.maximum(0, (low_first - base + 2 * TILE - TILE) // (2 * TILE))
            stop = (first - base) // (2 * TILE) + 1

            def step(tile, _):
                position = base + tile * 2 * TILE
                place = source * TILES + tile
                whole = (position >= low_last) & (position + TILE - 1 <= first)

                @pl.when(whole)
                def _():
                    visit(place, None)

                @pl.when(jnp.logical_not(whole))
                def _():
                    key = position + lax.broadcasted_iota(jnp.int32, (TILE, TILE), 1)
                    query = first + lax.broadcasted_iota(jnp.int32, (TILE, TILE), 0)
                    low = lows_ref[rows, :]
                    low = jnp.concatenate([low, low], 1)
                    visit(place, (key <= query) & (key >= low))

                return 0

            lax.fori_loop(start, stop, step, 0)

        for head in range(PER_GROUP):
            total = acc_s[head]
            out_ref[rows, head * HEAD : (head + 1) * HEAD] = (
                total[:, :HEAD] / total[:, HEAD:]
            ).astype(jnp.bfloat16)


def kernel(scalars, q_ref, lows_ref, *refs):
    own, other = refs[: BACK + 1], refs[BACK + 1 : 2 * (BACK + 1)]
    attend(scalars, q_ref, lows_ref, own, other, *refs[2 * (BACK + 1) :])


def call_kernel(scalars, q, lows, own, other):
    vmem = pl.BlockSpec(memory_space=pltpu.VMEM)
    return pl.pallas_call(
        kernel,
        out_shape=jax.ShapeDtypeStruct(q.shape, jnp.bfloat16),
        in_specs=[pl.BlockSpec(memory_space=pltpu.SMEM)] + [vmem] * (2 + len(own) + len(other)),
        out_specs=vmem,
        scratch_shapes=[
            pltpu.VMEM((2 * TILES, HEAD, TILE), jnp.bfloat16),
            pltpu.VMEM((2 * TILES, TILE, 2 * HEAD), jnp.bfloat16),
            pltpu.VMEM((PER_GROUP, TILE, HEAD), jnp.float32),
            pltpu.VMEM((PER_GROUP, TILE, 2 * HEAD), jnp.float32),
        ],
        compiler_params=pltpu.CompilerParams(vmem_limit_bytes=40 * 1024 * 1024),
        cost_estimate=pl.CostEstimate(
            flops=2 * 2 * 2560 * 4096 * 128, bytes_accessed=8 << 20, transcendentals=2560 * 4096
        ),
        name="attention",
    )(scalars, q, lows, *own, *other)


def bounds(index, core, lengths):
    starts = jnp.cumsum(lengths) - lengths
    firsts = index * SUPER + core * TILE + jnp.arange(2, dtype=jnp.int32) * 2 * TILE
    query = (firsts[:, None] + jnp.arange(TILE, dtype=jnp.int32)[None, :]).reshape(2 * TILE)
    low = jnp.max(jnp.where(starts[None, :] <= query[:, None], starts[None, :], 0), 1)
    lows = jnp.broadcast_to(low[:, None], (2 * TILE, HEAD))
    base = (index - BACK) * SUPER
    bases = jnp.stack([base + core * TILE, base + (1 - core) * TILE])
    scalars = jnp.concatenate([firsts, low[::TILE], low[TILE - 1 :: TILE], bases])
    return scalars.astype(jnp.int32), lows.astype(jnp.int32)


def local(queries, keys, values, lengths):
    rows = keys.shape[0]
    pair = jnp.stack([keys.reshape(rows, GROUPS, HEAD), values.reshape(rows, GROUPS, HEAD)], 2)
    pair = pair.reshape(rows, GROUPS * 2 * HEAD)
    chain = ("y", "w", "X")
    heads = ("l", "d")
    own = lax.all_to_all(pair, heads, split_axis=1, concat_axis=0, tiled=True)
    q = lax.all_to_all(queries, heads, split_axis=1, concat_axis=0, tiled=True)
    length = lax.axis_size("y") * 4
    held = [own]
    for distance in range(1, BACK + 1):
        route = [(i, i + distance) for i in range(length - distance)]
        held.append(lax.ppermute(own, chain, route))
    held = held[::-1]
    swapped = lax.ppermute(jnp.stack(held), "c", [(0, 1), (1, 0)])
    other = [swapped[i] for i in range(BACK + 1)]
    index = lax.axis_index(chain)
    scalars, lows = bounds(index, lax.axis_index("c"), lengths)
    out = call_kernel(scalars, q, lows, held, other)
    return lax.all_to_all(out, heads, split_axis=0, concat_axis=1, tiled=True)


def solution(mesh):
    fine = Mesh(mesh.devices.reshape(8, 2, 2, 2, 2, 4), ("y", "w", "X", "l", "c", "d"))
    rows = P(("y", "w", "X", "l", "c", "d"), None)
    return jax.shard_map(
        local, mesh=fine, in_specs=(rows, rows, rows, P()), out_specs=rows, check_vma=False
    )
```

time: 336 us -> 125 us (0.37)
  the two profiles are of different devices: /device:TPU:32 before, /device:TPU:25 now
where the time goes in v1:
time: 125 us; the launch traced here: 124 us
  blocking collectives  39.4 us (32%)
  waiting for transfers between devices  26.5 us (21%)
  starting transfers between devices  24.6 us (20%)
  Pallas kernels  23.7 us (19%)
  local copies, waits for them, and re-layouts  9.6 us (8%)
    pallas_call x1, Pallas kernels, call_kernel(): pl.pallas_call(kernel, out_shape=jax.ShapeDtypeStruct(q.shape, jnp.bfloat...  23.7 us
    all_to_all x1, blocking collectives, local(): return lax.all_to_all(out, heads, split_axis=0, concat_axis=1, tiled=True)  20 us
    all_to_all x1, blocking collectives, local(): own = lax.all_to_all(pair, heads, split_axis=1, concat_axis=0, tiled=True)  19.4 us
    ppermute x4, starting transfers between devices, local(): held.append(lax.ppermute(own, chain, route))  17.3 us
    all_to_all x1, waiting for transfers between devices, local(): q = lax.all_to_all(queries, heads, split_axis=1, concat_axis=0, tiled=True)  14.5 us
    ppermute x4, waiting for transfers between devices, local(): held.append(lax.ppermute(own, chain, route))  12 us
    unnamed x11, local copies, waits for them, and re-layouts  4.79 us
    ppermute x1, starting transfers between devices, local(): swapped = lax.ppermute(jnp.stack(held), 'c', [(0, 1), (1, 0)])  3.81 us
  transfers between devices with their start and end apart: 6, of which 3 were waited for; matrix products, arithmetic and copies ran while one was open for 4% of the time, Pallas kernels for 0%

profile of v1, /device:TPU:25, one launch (start us, length us, event | category | flops | bytes accessed | tf_op | source)
XLA Modules:
  0.0 124.4 jit_solution(15312440116161076022)
XLA Ops:
  0.0 0.9 copy.20
  0.9 0.9 copy.21
  1.9 0.3 copy.15
  2.2 0.2 all_to_all.46
  2.3 19.4 %all_to_all.57 = bf16[64,8,256]{2,0,1:T(8,128)(2,1)S(1)} all-to-all(bf16[64,8,256]{2,0,1:T(8,128)(2,1)S(1)} %all_to_all.46), channel_id=1, replica_groups=mesh['y'=8,'w'=2,'X'=2,'l'=2,'c'=2,'d'=4] {'l','d'}, dimensions={1} | all-to-all | bytes 524288 | tf_op jit(solution)/shard_map/all_to_all | solution.py:134
  21.7 4.5 %collective-permute-start = (bf16[512,256]{1,0:T(8,128)(2,1)S(1)}, bf16[512,256]{1,0:T(8,128)(2,1)S(1)}, u32[]{:S(2)}, u32[]{:S(2)}) collective-permute-start(bf16[512,256]{1,0:T(8,128)(2,1)S(1)} %bitcast.50), channel_id=1, source_target_pairs={{0,64},{16,80},{32,96},{48,112},{64,128},{80,144},{96,160},{112,17... | collective-permute-start | bytes 786440 | tf_op jit(solution)/shard_map/ppermute | solution.py:140
  26.3 8.0 %collective-permute-start.1 = (bf16[512,256]{1,0:T(8,128)(2,1)S(1)}, bf16[512,256]{1,0:T(8,128)(2,1)S(1)}, u32[]{:S(2)}, u32[]{:S(2)}) collective-permute-start(bf16[512,256]{1,0:T(8,128)(2,1)S(1)} %bitcast.51), channel_id=1, source_target_pairs={{0,48},{16,64},{32,80},{48,96},{64,112},{80,128},{96,144},{112,160... | collective-permute-start | bytes 786440 | tf_op jit(solution)/shard_map/ppermute | solution.py:140
  34.3 1.9 %collective-permute-start.2 = (bf16[512,256]{1,0:T(8,128)(2,1)S(1)}, bf16[512,256]{1,0:T(8,128)(2,1)S(1)}, u32[]{:S(2)}, u32[]{:S(2)}) collective-permute-start(bf16[512,256]{1,0:T(8,128)(2,1)S(1)} %bitcast.52), channel_id=1, source_target_pairs={{0,32},{16,48},{32,64},{48,80},{64,96},{80,112},{96,128},{112,144}... | collective-permute-start | bytes 786440 | tf_op jit(solution)/shard_map/ppermute | solution.py:140
  36.2 2.8 %collective-permute-start.3 = (bf16[512,256]{1,0:T(8,128)(2,1)S(1)}, bf16[512,256]{1,0:T(8,128)(2,1)S(1)}, u32[]{:S(2)}, u32[]{:S(2)}) collective-permute-start(bf16[512,256]{1,0:T(8,128)(2,1)S(1)} %bitcast.53), channel_id=1, source_target_pairs={{0,16},{16,32},{32,48},{48,64},{64,80},{80,96},{96,112},{112,128},... | collective-permute-start | bytes 786440 | tf_op jit(solution)/shard_map/ppermute | solution.py:140
  39.0 0.7 bitcast_dynamic-update-slice_fusion.3
  39.8 0.7 bitcast_dynamic-update-slice_fusion.2
  40.5 5.0 %collective-permute-done.2.refs_2_ = bf16[512,256]{1,0:T(8,128)(2,1)S(1)} collective-permute-done((bf16[512,256]{1,0:T(8,128)(2,1)S(1)}, bf16[512,256]{1,0:T(8,128)(2,1)S(1)}, u32[]{:S(2)}, u32[]{:S(2)}) %collective-permute-start.2) | collective-permute-done | bytes 262176 | tf_op jit(solution)/shard_map/ppermute | solution.py:140
  45.5 0.7 bitcast_dynamic-update-slice_fusion.1
  46.2 7.0 %collective-permute-done.3.refs_3_ = bf16[512,256]{1,0:T(8,128)(2,1)S(1)} collective-permute-done((bf16[512,256]{1,0:T(8,128)(2,1)S(1)}, bf16[512,256]{1,0:T(8,128)(2,1)S(1)}, u32[]{:S(2)}, u32[]{:S(2)}) %collective-permute-start.3) | collective-permute-done | bytes 262176 | tf_op jit(solution)/shard_map/ppermute | solution.py:140
  53.2 0.8 bitcast_dynamic-update-slice_fusion
  54.0 0.7 constant_dynamic-update-slice_fusion
  54.7 3.8 %collective-permute-start.4 = (bf16[5,512,256]{2,1,0:T(8,128)(2,1)}, bf16[5,512,256]{2,1,0:T(8,128)(2,1)}, u32[]{:S(2)}, u32[]{:S(2)}) collective-permute-start(bf16[5,512,256]{2,1,0:T(8,128)(2,1)} %constant_dynamic-update-slice_fusion), channel_id=1, source_target_pairs={{0,4},{4,0},{1,5},{5,1},{2,6},{6,2},{3,7},{7,3},{8,12},{12,8},{9,1... | collective-permute-start | bytes 3932168 | tf_op jit(solution)/shard_map/ppermute | solution.py:142
  58.5 0.9 copy.23
  59.4 3.5 %all-to-all-start = ((bf16[64,8,640]{2,0,1:T(8,128)(2,1)}), bf16[64,8,640]{2,0,1:T(8,128)(2,1)S(1)}, u32[]{:S(2)}, u32[]{:S(2)}) async-start(bf16[64,8,640]{2,0,1:T(8,128)(2,1)} %bitcast.49), calls=%async_computation | async-start | bytes 1310720 | tf_op jit(solution)/shard_map/all_to_all | solution.py:135
  63.8 1.4 %slice_bitcast_fusion = (bf16[512,256]{1,0:T(8,128)(2,1)S(1)}, bf16[512,256]{1,0:T(8,128)(2,1)S(1)}, bf16[512,256]{1,0:T(8,128)(2,1)S(1)}, bf16[512,256]{1,0:T(8,128)(2,1)S(1)}, bf16[512,256]{1,0:T(8,128)(2,1)S(1)}) fusion(bf16[5,512,256]{2,1,0:T(8,128)(2,1)} %collective-permute-done.4), kind=kLoop, calls=%fused_computation.1 | loop fusion | bytes 2621440 | tf_op jit(solution)/shard_map/squeeze | solution.py:143
  65.1 14.5 %all-to-all-done = bf16[64,8,640]{2,0,1:T(8,128)(2,1)S(1)} async-done(((bf16[64,8,640]{2,0,1:T(8,128)(2,1)}), bf16[64,8,640]{2,0,1:T(8,128)(2,1)S(1)}, u32[]{:S(2)}, u32[]{:S(2)}) %all-to-all-start) | async-done | bytes 655392 | tf_op jit(solution)/shard_map/all_to_all | solution.py:135
  79.7 23.7 %attention.1 = bf16[512,640]{1,0:T(8,128)(2,1)S(1)} custom-call(s32[8]{0:T(128)S(1)} %concatenate.3.scalars, bf16[512,640]{1,0:T(8,128)(2,1)S(1)} %bitcast.56, s32[512,128]{1,0:T(8,128)S(1)} %broadcast_in_dim.13.lows_ref, bf16[512,256]{1,0:T(8,128)(2,1)S(1)} %collective-permute-done.refs_0_, bf16[512,256]{1,0:T(8,128)(2,1)S(1)} %collective-permute-done.1.refs_1_, ...), custom_call_target="tpu_custom_call" | custom-call | flops 5368709120 | bytes 8388608 | tf_op jit(solution)/shard_map/attention/pallas_call | solution.py:97
  103.5 20.0 %all_to_all.58 = bf16[8,64,640]{2,1,0:T(8,128)(2,1)S(1)} all-to-all(bf16[8,64,640]{2,1,0:T(8,128)(2,1)S(1)} %bitcast.57), channel_id=1, replica_groups=mesh['y'=8,'w'=2,'X'=2,'l'=2,'c'=2,'d'=4] {'l','d'}, dimensions={0} | all-to-all | bytes 1310720 | tf_op jit(solution)/shard_map/all_to_all | solution.py:147
  123.5 0.9 copy.18
  (20 shorter events, 0.9 us)
Async XLA Ops:
  21.7 36.8 %copy-start = (bf16[64,5120]{1,0:T(8,128)(2,1)S(1)}, bf16[64,5120]{1,0:T(8,128)(2,1)}, u32[]{:S(2)}) copy-start(bf16[64,5120]{1,0:T(8,128)(2,1)} %param.4) | copy-start | bytes 1966084
  21.7 17.3 %collective-permute-start = (bf16[512,256]{1,0:T(8,128)(2,1)S(1)}, bf16[512,256]{1,0:T(8,128)(2,1)S(1)}, u32[]{:S(2)}, u32[]{:S(2)}) collective-permute-start(bf16[512,256]{1,0:T(8,128)(2,1)S(1)} %bitcast.50), channel_id=1, source_target_pairs={{0,64},{16,80},{32,96},{48,112},{64,128},{80,144},{96,160},{112,17... | collective-permute-start | bytes 786440 | tf_op jit(solution)/shard_map/ppermute | solution.py:140
  26.3 13.5 %collective-permute-start.1 = (bf16[512,256]{1,0:T(8,128)(2,1)S(1)}, bf16[512,256]{1,0:T(8,128)(2,1)S(1)}, u32[]{:S(2)}, u32[]{:S(2)}) collective-permute-start(bf16[512,256]{1,0:T(8,128)(2,1)S(1)} %bitcast.51), channel_id=1, source_target_pairs={{0,48},{16,64},{32,80},{48,96},{64,112},{80,128},{96,144},{112,160... | collective-permute-start | bytes 786440 | tf_op jit(solution)/shard_map/ppermute | solution.py:140
  34.3 11.2 %collective-permute-start.2 = (bf16[512,256]{1,0:T(8,128)(2,1)S(1)}, bf16[512,256]{1,0:T(8,128)(2,1)S(1)}, u32[]{:S(2)}, u32[]{:S(2)}) collective-permute-start(bf16[512,256]{1,0:T(8,128)(2,1)S(1)} %bitcast.52), channel_id=1, source_target_pairs={{0,32},{16,48},{32,64},{48,80},{64,96},{80,112},{96,128},{112,144}... | collective-permute-start | bytes 786440 | tf_op jit(solution)/shard_map/ppermute | solution.py:140
  36.2 17.0 %collective-permute-start.3 = (bf16[512,256]{1,0:T(8,128)(2,1)S(1)}, bf16[512,256]{1,0:T(8,128)(2,1)S(1)}, u32[]{:S(2)}, u32[]{:S(2)}) collective-permute-start(bf16[512,256]{1,0:T(8,128)(2,1)S(1)} %bitcast.53), channel_id=1, source_target_pairs={{0,16},{16,32},{32,48},{48,64},{64,80},{80,96},{96,112},{112,128},... | collective-permute-start | bytes 786440 | tf_op jit(solution)/shard_map/ppermute | solution.py:140
  54.7 9.1 %collective-permute-start.4 = (bf16[5,512,256]{2,1,0:T(8,128)(2,1)}, bf16[5,512,256]{2,1,0:T(8,128)(2,1)}, u32[]{:S(2)}, u32[]{:S(2)}) collective-permute-start(bf16[5,512,256]{2,1,0:T(8,128)(2,1)} %constant_dynamic-update-slice_fusion), channel_id=1, source_target_pairs={{0,4},{4,0},{1,5},{5,1},{2,6},{6,2},{3,7},{7,3},{8,12},{12,8},{9,1... | collective-permute-start | bytes 3932168 | tf_op jit(solution)/shard_map/ppermute | solution.py:142
  58.5 4.6 %copy-start.1 = (s32[48]{0:T(128)S(1)}, s32[48]{0:T(128)}, u32[]{:S(2)}) copy-start(s32[48]{0:T(128)} %param.7) | copy-start | bytes 580
  59.4 20.1 %all-to-all-start = ((bf16[64,8,640]{2,0,1:T(8,128)(2,1)}), bf16[64,8,640]{2,0,1:T(8,128)(2,1)S(1)}, u32[]{:S(2)}, u32[]{:S(2)}) async-start(bf16[64,8,640]{2,0,1:T(8,128)(2,1)} %bitcast.49), calls=%async_computation | async-start | bytes 1310720 | tf_op jit(solution)/shard_map/all_to_all | solution.py:135

commit v2 on v0

v2 whole, which is shorter than its diff:
```python
import functools
import math

import jax
import jax.numpy as jnp
from jax import lax
from jax.experimental import pallas as pl
from jax.experimental.pallas import tpu as pltpu
from jax.sharding import Mesh, PartitionSpec as P

HEAD = 128
HEADS = 40
GROUPS = 8
PER_GROUP = HEADS // GROUPS
PART = 256
TILE = 2 * PART
SUPER = 2 * TILE
ROWS = PER_GROUP * PART
SCALE = math.log2(math.e) / math.sqrt(HEAD)
LOWEST = -1e30


def double(x, times=2):
    return jnp.concatenate([x] * times, 1)


def visit(q, kt, v, m_ref, acc_ref, allowed):
    scores = jnp.dot(q, kt, preferred_element_type=jnp.float32)
    weights, decay = [], []
    for head in range(PER_GROUP):
        rows = slice(head * PART, (head + 1) * PART)
        scaled = scores[rows] * SCALE
        if allowed is not None:
            scaled = jnp.where(allowed, scaled, LOWEST)
        m_old = m_ref[rows]
        m_new = jnp.maximum(m_old, jnp.max(scaled, 1, keepdims=True))
        m_ref[rows] = m_new
        decay.append(jnp.exp2(m_old - m_new))
        weights.append(jnp.exp2(scaled - double(m_new, TILE // HEAD)).astype(jnp.bfloat16))
    part = jnp.dot(jnp.concatenate(weights, 0), v, preferred_element_type=jnp.float32)
    for head in range(PER_GROUP):
        rows = slice(head * PART, (head + 1) * PART)
        acc_ref[rows] = acc_ref[rows] * double(decay[head]) + part[rows]


def load(own_refs, other_refs, kt_s, v_s):
    tile = 0
    for own, other in zip(own_refs, other_refs):
        for half in range(2):
            rows = slice(half * PART, (half + 1) * PART)
            for source, ref in enumerate((own, other)):
                span = slice(source * PART, (source + 1) * PART)
                kt_s[tile, :, span] = ref[rows, :HEAD].T
                v_s[tile, span, :HEAD] = ref[rows, HEAD:]
                v_s[tile, span, HEAD:] = jnp.ones((PART, HEAD), jnp.bfloat16)
            tile += 1


def sweep(scalars, block, slots, q_s, lows_ref, kt_s, v_s, m_ref, acc_ref):
    first = scalars[block]
    low_first = scalars[2 + block]
    low_last = scalars[4 + block]
    core = scalars[6]
    rows = pl.ds(pl.multiple_of(block * PART, PART), PART)
    for place, slot in enumerate(slots):
        base = scalars[7 + slot]
        start = jnp.clip((low_first - base) // TILE, 0, 2)
        stop = jnp.clip((first + PART - 1 - base) // TILE + 1, 0, 2)

        def step(tile, _):
            position = base + tile * TILE
            whole = (position >= low_last) & (position + TILE - 1 <= first)

            def go(allowed):
                kt, v = kt_s[2 * place + tile], v_s[2 * place + tile]
                visit(q_s[block], kt, v, m_ref.at[block], acc_ref.at[block], allowed)

            @pl.when(whole)
            def _():
                go(None)

            @pl.when(jnp.logical_not(whole))
            def _():
                column = lax.broadcasted_iota(jnp.int32, (PART, TILE), 1)
                key = position + jnp.bitwise_xor(column, core * PART)
                query = first + lax.broadcasted_iota(jnp.int32, (PART, TILE), 0)
                low = double(lows_ref[rows, :], TILE // HEAD)
                go((key <= query) & (key >= low))

            return 0

        lax.fori_loop(start, stop, step, 0)


def stack_heads(q_ref, q_s):
    for block in range(2):
        for head in range(PER_GROUP):
            q_s[block, head * PART : (head + 1) * PART] = q_ref[
                block * PART : (block + 1) * PART, head * HEAD : (head + 1) * HEAD
            ]


def fold_kernel(slots, first, last, scalars, q_ref, lows_ref, *refs):
    count = len(slots)
    own, other, refs = refs[0], refs[1], refs[2:]
    if not first:
        m_in, acc_in, refs = refs[0], refs[1], refs[2:]
    if last:
        out_ref, refs = refs[0], refs[1:]
    m_ref, acc_ref, q_s, kt_s, v_s = refs
    stack_heads(q_ref, q_s)
    load([own.at[i] for i in range(count)], [other.at[i] for i in range(count)], kt_s, v_s)
    if first:
        m_ref[...] = jnp.full(m_ref.shape, LOWEST, jnp.float32)
        acc_ref[...] = jnp.zeros(acc_ref.shape, jnp.float32)
    else:
        m_ref[...] = m_in[...]
        acc_ref[...] = acc_in[...]

    def one(block, _):
        sweep(scalars, block, slots, q_s, lows_ref, kt_s, v_s, m_ref, acc_ref)
        if last:
            rows = pl.ds(pl.multiple_of(block * PART, PART), PART)
            for head in range(PER_GROUP):
                total = acc_ref[block, head * PART : (head + 1) * PART]
                out_ref[rows, head * HEAD : (head + 1) * HEAD] = (
                    total[:, :HEAD] / total[:, HEAD:]
                ).astype(jnp.bfloat16)
        return 0

    lax.fori_loop(0, 2, one, 0)


def specs(count):
    return [pl.BlockSpec(memory_space=pltpu.SMEM)] + [pl.BlockSpec(memory_space=pltpu.VMEM)] * count


def scratch(tiles):
    return [
        pltpu.VMEM((2, ROWS, HEAD), jnp.bfloat16),
        pltpu.VMEM((tiles, HEAD, TILE), jnp.bfloat16),
        pltpu.VMEM((tiles, TILE, 2 * HEAD), jnp.bfloat16),
    ]


def cost(tiles):
    pairs = 2 * ROWS * tiles * TILE
    return pl.CostEstimate(flops=4 * HEAD * pairs, bytes_accessed=4 << 20, transcendentals=pairs)


STATE = (
    jax.ShapeDtypeStruct((2, ROWS, HEAD), jnp.float32),
    jax.ShapeDtypeStruct((2, ROWS, 2 * HEAD), jnp.float32),
)
PARAMS = pltpu.CompilerParams(vmem_limit_bytes=32 * 1024 * 1024)


def fold(slots, scalars, q, lows, own, other, state=(), last=False):
    count = len(slots)
    vmem = pl.BlockSpec(memory_space=pltpu.VMEM)
    keep = [pltpu.VMEM(s.shape, s.dtype) for s in STATE] if last else []
    return pl.pallas_call(
        functools.partial(fold_kernel, slots, not state, last),
        out_shape=jax.ShapeDtypeStruct(q.shape, jnp.bfloat16) if last else STATE,
        in_specs=specs(4 + len(state)),
        out_specs=vmem if last else [vmem] * 2,
        scratch_shapes=keep + scratch(2 * count),
        compiler_params=PARAMS,
        cost_estimate=cost(2 * count),
        name="attend_%d" % slots[0],
    )(scalars, q, lows, own, other, *state)


def bounds(index, core, lengths):
    starts = jnp.cumsum(lengths) - lengths
    firsts = index * SUPER + core * PART + jnp.arange(2, dtype=jnp.int32) * TILE
    query = (firsts[:, None] + jnp.arange(PART, dtype=jnp.int32)[None, :]).reshape(TILE)
    low = jnp.max(jnp.where(starts[None, :] <= query[:, None], starts[None, :], 0), 1)
    lows = jnp.broadcast_to(low[:, None], (TILE, HEAD))
    bases = [index, index - 2, index - 4, index - 1, index - 3]
    place = jnp.stack([core] + [base * SUPER for base in bases])
    scalars = jnp.concatenate([firsts, low[::PART], low[PART - 1 :: PART], place])
    return scalars.astype(jnp.int32), lows.astype(jnp.int32)


def forward(block, axes, distance):
    size = math.prod(lax.axis_size(axis) for axis in axes)
    return lax.ppermute(block, axes, [(i, i + distance) for i in range(size - distance)])


def flip(block, axis):
    return lax.ppermute(block, axis, [(0, 1), (1, 0)])


def local(queries, keys, values, lengths):
    rows = keys.shape[0]
    pair = jnp.stack([keys.reshape(rows, GROUPS, HEAD), values.reshape(rows, GROUPS, HEAD)], 2)
    pair = pair.reshape(rows, GROUPS * 2 * HEAD)
    chain = ("y", "w", "X")
    heads = ("l", "d")
    index, core = lax.axis_index(chain), lax.axis_index("c")
    scalars, lows = bounds(index, core, lengths)
    own = lax.all_to_all(pair, heads, split_axis=1, concat_axis=0, tiled=True)
    q = lax.all_to_all(queries, heads, split_axis=1, concat_axis=0, tiled=True)
    near = jnp.stack([own, forward(own, chain, 2), forward(own, chain, 4)])
    send = lax.dynamic_slice_in_dim(near, lax.axis_index("X"), 2, 0)
    distant = flip(send, "X")
    m, acc = fold((0, 1, 2), scalars, q, lows, near, flip(near, "c"))
    distant, m = lax.optimization_barrier((distant, m))
    out = fold((3, 4), scalars, q, lows, distant, flip(distant, "c"), (m, acc), last=True)
    return lax.all_to_all(out, heads, split_axis=0, concat_axis=1, tiled=True)


def solution(mesh):
    fine = Mesh(mesh.devices.reshape(8, 2, 2, 2, 2, 4), ("y", "w", "X", "l", "c", "d"))
    rows = P(("y", "w", "X", "l", "c", "d"), None)
    return jax.shard_map(
        local, mesh=fine, in_specs=(rows, rows, rows, P()), out_specs=rows, check_vma=False
    )
```

time: 336 us -> 98.1 us (0.29)
  the two profiles are of different devices: /device:TPU:32 before, /device:TPU:6 now
where the time goes in v2:
time: 98.1 us; the launch traced here: 97.7 us
  blocking collectives  48.2 us (49%)
  starting transfers between devices  19.2 us (20%)
  waiting for transfers between devices  14.6 us (15%)
  Pallas kernels  10.3 us (10%)
  local copies, waits for them, and re-layouts  4.7 us (5%)
    all_to_all x1, blocking collectives, local(): return lax.all_to_all(out, heads, split_axis=0, concat_axis=1, tiled=True)  26.1 us
    all_to_all x1, blocking collectives, local(): own = lax.all_to_all(pair, heads, split_axis=1, concat_axis=0, tiled=True)  22.1 us
    all_to_all x1, waiting for transfers between devices, local(): q = lax.all_to_all(queries, heads, split_axis=1, concat_axis=0, tiled=True)  11.3 us
    pallas_call x2, Pallas kernels, fold(): pl.pallas_call(functools.partial(fold_kernel, slots, not state, last), ou...  10.3 us
    ppermute x3, starting transfers between devices, flip(): return lax.ppermute(block, axis, [(0, 1), (1, 0)])  7.32 us
    ppermute x2, starting transfers between devices, forward(): lax.ppermute(block, axes, [(i, i + distance) for i in range(size - distan...  6.13 us
    all_to_all x1, starting transfers between devices, local(): q = lax.all_to_all(queries, heads, split_axis=1, concat_axis=0, tiled=True)  5.71 us
    ppermute x3, waiting for transfers between devices, flip(): return lax.ppermute(block, axis, [(0, 1), (1, 0)])  3.37 us
  transfers between devices with their start and end apart: 6, of which 3 were waited for; matrix products, arithmetic and copies ran while one was open for 2% of the time, Pallas kernels for 5%

profile of v2, /device:TPU:6, one launch (start us, length us, event | category | flops | bytes accessed | tf_op | source)
XLA Modules:
  0.0 97.7 jit_solution(15443661470785730640)
XLA Ops:
  0.0 1.0 %copy.20 = bf16[8,8,8,128]{3,2,1,0:T(8,128)(2,1)S(1)} copy(bf16[8,8,8,128]{3,1,2,0:T(8,128)(2,1)} %bitcast.50) | data formatting | bytes 262144
  1.0 0.9 copy.21
  2.0 0.3 copy.15
  2.2 0.2 all_to_all.46
  2.4 22.1 %all_to_all.57 = bf16[64,8,256]{2,0,1:T(8,128)(2,1)S(1)} all-to-all(bf16[64,8,256]{2,0,1:T(8,128)(2,1)S(1)} %all_to_all.46), channel_id=1, replica_groups=mesh['y'=8,'w'=2,'X'=2,'l'=2,'c'=2,'d'=4] {'l','d'}, dimensions={1} | all-to-all | bytes 524288 | tf_op jit(solution)/shard_map/all_to_all | solution.py:203
  24.5 2.6 %collective-permute-start = (bf16[512,256]{1,0:T(8,128)(2,1)S(1)}, bf16[512,256]{1,0:T(8,128)(2,1)S(1)}, u32[]{:S(2)}, u32[]{:S(2)}) collective-permute-start(bf16[512,256]{1,0:T(8,128)(2,1)S(1)} %bitcast.42), channel_id=1, source_target_pairs={{0,32},{16,48},{32,64},{48,80},{64,96},{80,112},{96,128},{112,144}... | collective-permute-start | bytes 786440 | tf_op jit(solution)/shard_map/ppermute | solution.py:188
  27.2 3.5 %collective-permute-start.1 = (bf16[512,256]{1,0:T(8,128)(2,1)S(1)}, bf16[512,256]{1,0:T(8,128)(2,1)S(1)}, u32[]{:S(2)}, u32[]{:S(2)}) collective-permute-start(bf16[512,256]{1,0:T(8,128)(2,1)S(1)} %bitcast.43), channel_id=1, source_target_pairs={{0,64},{16,80},{32,96},{48,112},{64,128},{80,144},{96,160},{112,17... | collective-permute-start | bytes 786440 | tf_op jit(solution)/shard_map/ppermute | solution.py:188
  30.7 0.9 copy.23
  31.6 5.7 %all-to-all-start = ((bf16[64,8,640]{2,0,1:T(8,128)(2,1)}), bf16[64,8,640]{2,0,1:T(8,128)(2,1)S(1)}, u32[]{:S(2)}, u32[]{:S(2)}) async-start(bf16[64,8,640]{2,0,1:T(8,128)(2,1)} %bitcast.37), calls=%async_computation | async-start | bytes 1310720 | tf_op jit(solution)/shard_map/all_to_all | solution.py:204
  37.4 1.9 %collective-permute-start.3 = (bf16[3,512,256]{2,1,0:T(8,128)(2,1)S(1)}, bf16[3,512,256]{2,1,0:T(8,128)(2,1)S(1)}, u32[]{:S(2)}, u32[]{:S(2)}) collective-permute-start(bf16[3,512,256]{2,1,0:T(8,128)(2,1)S(1)} %pad_maximum_fusion.refs_0_), channel_id=1, source_target_pairs={{0,4},{4,0},{1,5},{5,1},{2,6},{6,2},{3,7},{7,3},{8,12},{12,8},{9,1... | collective-permute-start | bytes 2359304 | tf_op jit(solution)/shard_map/ppermute | solution.py:192
  39.4 3.3 %collective-permute-start.2 = (bf16[2,512,256]{2,1,0:T(8,128)(2,1)S(1)}, bf16[2,512,256]{2,1,0:T(8,128)(2,1)S(1)}, u32[]{:S(2)}, u32[]{:S(2)}) collective-permute-start(bf16[2,512,256]{2,1,0:T(8,128)(2,1)S(1)} %constant_dynamic-slice_fusion), channel_id=1, source_target_pairs={{0,16},{16,0},{1,17},{17,1},{2,18},{18,2},{3,19},{19,3},{4,20},{20... | collective-permute-start | bytes 1572872 | tf_op jit(solution)/shard_map/ppermute | solution.py:192
  43.0 0.1 reduce
  43.1 0.1 select_reduce_fusion
  43.2 0.1 slice.6
  43.3 0.1 slice.7
  43.5 11.3 %all-to-all-done = bf16[64,8,640]{2,0,1:T(8,128)(2,1)S(1)} async-done(((bf16[64,8,640]{2,0,1:T(8,128)(2,1)}), bf16[64,8,640]{2,0,1:T(8,128)(2,1)S(1)}, u32[]{:S(2)}, u32[]{:S(2)}) %all-to-all-start) | async-done | bytes 655392 | tf_op jit(solution)/shard_map/all_to_all | solution.py:204
  54.8 0.1 broadcast_in_dim.13.lows_ref
  54.9 5.0 %attend_0.1 = (f32[2,1280,128]{2,1,0:T(8,128)S(1)}, f32[2,1280,256]{2,1,0:T(8,128)S(1)}) custom-call(s32[12]{0:T(128)S(1)} %concatenate.3.scalars, bf16[512,640]{1,0:T(8,128)(2,1)S(1)} %bitcast.38, s32[512,128]{1,0:T(8,128)S(1)} %broadcast_in_dim.13.lows_ref, bf16[3,512,256]{2,1,0:T(8,128)(2,1)S(1)} %pad_maximum_fusion.refs_0_, ...), custom_call_target="tpu_custom_call" | custom-call | flops 4026531840 | bytes 4194304 | tf_op jit(solution)/shard_map/attend_0/pallas_call | solution.py:162
  59.9 1.7 %collective-permute-done.2.refs_0_ = bf16[2,512,256]{2,1,0:T(8,128)(2,1)S(1)} collective-permute-done((bf16[2,512,256]{2,1,0:T(8,128)(2,1)S(1)}, bf16[2,512,256]{2,1,0:T(8,128)(2,1)S(1)}, u32[]{:S(2)}, u32[]{:S(2)}) %collective-permute-start.2) | collective-permute-done | bytes 524320 | tf_op jit(solution)/shard_map/ppermute | solution.py:192
  61.6 2.1 %collective-permute-start.4 = (bf16[2,512,256]{2,1,0:T(8,128)(2,1)S(1)}, bf16[2,512,256]{2,1,0:T(8,128)(2,1)S(1)}, u32[]{:S(2)}, u32[]{:S(2)}) collective-permute-start(bf16[2,512,256]{2,1,0:T(8,128)(2,1)S(1)} %collective-permute-done.2.refs_0_), channel_id=1, source_target_pairs={{0,4},{4,0},{1,5},{5,1},{2,6},{6,2},{3,7},{7,3},{8,12},{12,8},{9,1... | collective-permute-start | bytes 1572872 | tf_op jit(solution)/shard_map/ppermute | solution.py:192
  63.6 1.7 %collective-permute-done.4.refs_1_ = bf16[2,512,256]{2,1,0:T(8,128)(2,1)S(1)} collective-permute-done((bf16[2,512,256]{2,1,0:T(8,128)(2,1)S(1)}, bf16[2,512,256]{2,1,0:T(8,128)(2,1)S(1)}, u32[]{:S(2)}, u32[]{:S(2)}) %collective-permute-start.4) | collective-permute-done | bytes 524320 | tf_op jit(solution)/shard_map/ppermute | solution.py:192
  65.3 5.4 %attend_3.1 = bf16[512,640]{1,0:T(8,128)(2,1)S(1)} custom-call(s32[12]{0:T(128)S(1)} %concatenate.3.scalars, bf16[512,640]{1,0:T(8,128)(2,1)S(1)} %bitcast.39, s32[512,128]{1,0:T(8,128)S(1)} %broadcast_in_dim.13.lows_ref, bf16[2,512,256]{2,1,0:T(8,128)(2,1)S(1)} %collective-permute-done.2.refs_0_, bf16[2,512,256]{2,1,0:T(8,128)(2,1)S(1)} %collective-permute-done.4.refs_1_, ...), custom_call_target="tpu_custom_call" | custom-call | flops 2684354560 | bytes 4194304 | tf_op jit(solution)/shard_map/attend_3/pallas_call | solution.py:162
  70.7 26.1 %all_to_all.58 = bf16[8,64,640]{2,1,0:T(8,128)(2,1)S(1)} all-to-all(bf16[8,64,640]{2,1,0:T(8,128)(2,1)S(1)} %bitcast.40), channel_id=1, replica_groups=mesh['y'=8,'w'=2,'X'=2,'l'=2,'c'=2,'d'=4] {'l','d'}, dimensions={0} | all-to-all | bytes 1310720 | tf_op jit(solution)/shard_map/all_to_all | solution.py:211
  96.8 0.9 copy.18
  (17 shorter events, 0.5 us)
Async XLA Ops:
  0.0 30.7 %copy-start = (bf16[64,5120]{1,0:T(8,128)(2,1)S(1)}, bf16[64,5120]{1,0:T(8,128)(2,1)}, u32[]{:S(2)}) copy-start(bf16[64,5120]{1,0:T(8,128)(2,1)} %param.4) | copy-start | bytes 1966084
  24.5 12.8 %collective-permute-start = (bf16[512,256]{1,0:T(8,128)(2,1)S(1)}, bf16[512,256]{1,0:T(8,128)(2,1)S(1)}, u32[]{:S(2)}, u32[]{:S(2)}) collective-permute-start(bf16[512,256]{1,0:T(8,128)(2,1)S(1)} %bitcast.42), channel_id=1, source_target_pairs={{0,32},{16,48},{32,64},{48,80},{64,96},{80,112},{96,128},{112,144}... | collective-permute-start | bytes 786440 | tf_op jit(solution)/shard_map/ppermute | solution.py:188
  27.2 10.1 %collective-permute-start.1 = (bf16[512,256]{1,0:T(8,128)(2,1)S(1)}, bf16[512,256]{1,0:T(8,128)(2,1)S(1)}, u32[]{:S(2)}, u32[]{:S(2)}) collective-permute-start(bf16[512,256]{1,0:T(8,128)(2,1)S(1)} %bitcast.43), channel_id=1, source_target_pairs={{0,64},{16,80},{32,96},{48,112},{64,128},{80,144},{96,160},{112,17... | collective-permute-start | bytes 786440 | tf_op jit(solution)/shard_map/ppermute | solution.py:188
  30.7 12.1 %copy-start.1 = (s32[48]{0:T(128)S(1)}, s32[48]{0:T(128)}, u32[]{:S(2)}) copy-start(s32[48]{0:T(128)} %param.7) | copy-start | bytes 580
  31.6 23.2 %all-to-all-start = ((bf16[64,8,640]{2,0,1:T(8,128)(2,1)}), bf16[64,8,640]{2,0,1:T(8,128)(2,1)S(1)}, u32[]{:S(2)}, u32[]{:S(2)}) async-start(bf16[64,8,640]{2,0,1:T(8,128)(2,1)} %bitcast.37), calls=%async_computation | async-start | bytes 1310720 | tf_op jit(solution)/shard_map/all_to_all | solution.py:204
  37.4 17.3 %collective-permute-start.3 = (bf16[3,512,256]{2,1,0:T(8,128)(2,1)S(1)}, bf16[3,512,256]{2,1,0:T(8,128)(2,1)S(1)}, u32[]{:S(2)}, u32[]{:S(2)}) collective-permute-start(bf16[3,512,256]{2,1,0:T(8,128)(2,1)S(1)} %pad_maximum_fusion.refs_0_), channel_id=1, source_target_pairs={{0,4},{4,0},{1,5},{5,1},{2,6},{6,2},{3,7},{7,3},{8,12},{12,8},{9,1... | collective-permute-start | bytes 2359304 | tf_op jit(solution)/shard_map/ppermute | solution.py:192
  39.4 22.1 %collective-permute-start.2 = (bf16[2,512,256]{2,1,0:T(8,128)(2,1)S(1)}, bf16[2,512,256]{2,1,0:T(8,128)(2,1)S(1)}, u32[]{:S(2)}, u32[]{:S(2)}) collective-permute-start(bf16[2,512,256]{2,1,0:T(8,128)(2,1)S(1)} %constant_dynamic-slice_fusion), channel_id=1, source_target_pairs={{0,16},{16,0},{1,17},{17,1},{2,18},{18,2},{3,19},{19,3},{4,20},{20... | collective-permute-start | bytes 1572872 | tf_op jit(solution)/shard_map/ppermute | solution.py:192
  61.6 3.8 %collective-permute-start.4 = (bf16[2,512,256]{2,1,0:T(8,128)(2,1)S(1)}, bf16[2,512,256]{2,1,0:T(8,128)(2,1)S(1)}, u32[]{:S(2)}, u32[]{:S(2)}) collective-permute-start(bf16[2,512,256]{2,1,0:T(8,128)(2,1)S(1)} %collective-permute-done.2.refs_0_), channel_id=1, source_target_pairs={{0,4},{4,0},{1,5},{5,1},{2,6},{6,2},{3,7},{7,3},{8,12},{12,8},{9,1... | collective-permute-start | bytes 1572872 | tf_op jit(solution)/shard_map/ppermute | solution.py:192
